TPU v7x, 256 devices: a whole 4x4x8 slice. The times are simulated.
256 devices in a mesh: dp: 16 (over z, core), own: 16 (over x, y).
Axes of the slice: x: 4, y: 4, z: 8, core: 2. Of those that a mesh axis runs over, the one named last changes fastest.
Arguments:
- tokens: bfloat16 [512, 256, 1024], P(('dp', 'own')), may hold values from -6 to 6
- cotangent: bfloat16 [512, 256, 1024], P(('dp', 'own')), may hold values from -6 to 6
- lengths: int32 [512], P(('dp', 'own')), may hold values from 1 to 256, as said below
- norm_gain: float32 [1024], replicated, may hold values from 0.1 to 12
- weight_in: bfloat16 [1024, 4096], P('own'), may hold values from -0.1875 to 0.1875
- weight_out: bfloat16 [1024, 1024], P('own'), may hold values from -0.1875 to 0.1875
- moment_in: float32 [1024, 4096], P('own'), may hold values from -6 to 6
- square_in: float32 [1024, 4096], P('own'), may hold values from 0.25 to 4
- moment_out: float32 [1024, 1024], P('own'), may hold values from -6 to 6
- square_out: float32 [1024, 1024], P('own'), may hold values from 0.25 to 4
Outputs:
- new_weight_in: float32 [1024, 4096], P('own')
- new_moment_in: float32 [1024, 4096], P('own')
- new_square_in: float32 [1024, 4096], P('own')
- new_weight_out: float32 [1024, 1024], P('own')
- new_moment_out: float32 [1024, 1024], P('own')
- new_square_out: float32 [1024, 1024], P('own')
Inputs may be any that keep to these rules, and one draw needn't show every extreme that they name: `lengths`: the live events of a history are its first ones; some history holds 256.
All inputs are finite; a program needn't handle non-finite values.
Results may differ from a plain program's by a relative error of at most 0.004.
Values may be sent and summed in bfloat16 or wider, within the bound.
No kernel may reach another device: no remote copies, remote signals or barrier semaphores. Data moves between devices by JAX's collectives and lax.ppermute only.
A program may use at most 128 MiB of HBM per device.

v0:
```python
import jax
import jax.numpy as jnp
from jax import lax
from jax.sharding import PartitionSpec as P

HEADS = 4
BLK = 256


norm_eps = 1e-06
beta_first = 0.9
beta_second = 0.95
learn_rate = 0.01
step_number = 10.0
update_eps = 1e-08
ratio_eps = 1e-06


def rms_scale(values):
    return values * lax.rsqrt(jnp.mean(values * values, axis=-1, keepdims=True) + norm_eps)


def slot_loss(projected, cot_masked, length, weight_full):
    row_count = projected.shape[0]
    activated = jax.nn.silu(projected)
    gating, values, queries, key_part = jnp.split(activated, 4, axis=1)
    head_width = values.shape[1] // HEADS
    values = values.astype(jnp.bfloat16).reshape(row_count, HEADS, head_width)
    queries = queries.astype(jnp.bfloat16).reshape(row_count, HEADS, head_width)
    key_part = key_part.astype(jnp.bfloat16).reshape(row_count, HEADS, head_width)
    scores = jnp.einsum(
        "qhd,khd->hqk", queries, key_part, preferred_element_type=jnp.float32
    ) * head_width ** (-0.5)
    row_index = jnp.arange(row_count, dtype=jnp.int32)
    allowed = (row_index[None, :] <= row_index[:, None]) & (row_index[:, None] < length)
    attention = (jax.nn.silu(scores) * allowed.astype(jnp.float32)[None, :, :] / BLK).astype(
        jnp.bfloat16
    )
    mixed = jnp.einsum(
        "hqk,khd->qhd", attention, values, preferred_element_type=jnp.float32
    ).reshape(row_count, -1)
    gated = (rms_scale(mixed) * gating).astype(jnp.bfloat16)
    output = jnp.dot(gated, weight_full, preferred_element_type=jnp.float32)
    return (jnp.sum(output * cot_masked.astype(jnp.float32)), gated)


def slot_backward(projected, cot_masked, length, weight_full):

    def inner_loss(proj_rows):
        return slot_loss(proj_rows, cot_masked, length, weight_full)

    loss_value, pullback, gated = jax.vjp(inner_loss, projected, has_aux=True)
    grads = pullback(jnp.ones_like(loss_value))
    return (grads[0], gated)


def adam_parts(gradient, moment, square, clip_factor):
    scaled = gradient * clip_factor
    new_moment = beta_first * moment + (1.0 - beta_first) * scaled
    new_square = beta_second * square + (1.0 - beta_second) * scaled * scaled
    update = (
        new_moment
        / (1.0 - beta_first**step_number)
        / (jnp.sqrt(new_square / (1.0 - beta_second**step_number)) + update_eps)
    )
    return (new_moment, new_square, update)


def trust_step(weight, update, weight_sq, update_sq):
    trust_ratio = jnp.sqrt(weight_sq) / (jnp.sqrt(update_sq) + ratio_eps)
    return weight - learn_rate * trust_ratio[:, None] * update


def row_sums(values):
    return jnp.sum(values * values, axis=1)


def per_device(
    tokens,
    cotangent,
    lengths,
    norm_gain,
    weight_in,
    weight_out,
    moment_in,
    square_in,
    moment_out,
    square_out,
):
    slot_count, block_rows, model_width = tokens.shape
    normed = (rms_scale(tokens.astype(jnp.float32)) * norm_gain).astype(jnp.bfloat16)
    normed_rows = normed.reshape(slot_count * block_rows, model_width)
    weight_full = lax.all_gather(weight_out, "own", axis=0, tiled=True)
    row_index = jnp.arange(block_rows, dtype=jnp.int32)
    live_rows = row_index[None, :] < lengths[:, None]
    cot_masked = jnp.where(live_rows[:, :, None], cotangent, jnp.zeros_like(cotangent))
    columns = normed_rows
    projected = jnp.dot(
        columns,
        lax.all_gather(weight_in, "own", axis=0, tiled=True),
        preferred_element_type=jnp.float32,
    )
    projected = projected.reshape(slot_count, block_rows, -1)

    def one_slot(slot_items):
        grad_all, gated_all = slot_backward(
            slot_items[0], slot_items[1], slot_items[2], weight_full
        )
        return (grad_all.astype(jnp.bfloat16), gated_all)

    grad_projected, gated = lax.map(one_slot, (projected, cot_masked, lengths))
    grad_rows = grad_projected.reshape(slot_count * block_rows, -1)
    gated_rows = gated.reshape(-1, model_width)
    cot_rows = cot_masked.reshape(-1, model_width)
    columns = normed_rows
    part_in = lax.psum_scatter(
        jnp.dot(columns.T, grad_rows, preferred_element_type=jnp.float32).astype(jnp.bfloat16),
        "own",
        scatter_dimension=0,
        tiled=True,
    ).astype(jnp.float32)
    term_out = jnp.dot(gated_rows.T, cot_rows, preferred_element_type=jnp.float32)
    part_out = lax.psum_scatter(
        term_out.astype(jnp.bfloat16), "own", scatter_dimension=0, tiled=True
    ).astype(jnp.float32)
    grad_in, grad_out = lax.psum((part_in, part_out), "dp")
    local_square = jnp.sum(grad_in * grad_in) + jnp.sum(grad_out * grad_out)
    square_total = lax.psum(local_square, "own")
    clip_factor = jnp.minimum(
        1.0, jnp.sqrt(5.0 * model_width * model_width / (square_total + norm_eps))
    )
    new_moment_in, new_square_in, update_in = adam_parts(grad_in, moment_in, square_in, clip_factor)
    new_moment_out, new_square_out, update_out = adam_parts(
        grad_out, moment_out, square_out, clip_factor
    )
    weight_in_f = weight_in.astype(jnp.float32)
    weight_out_f = weight_out.astype(jnp.float32)
    new_weight_in = trust_step(weight_in_f, update_in, row_sums(weight_in_f), row_sums(update_in))
    new_weight_out = trust_step(
        weight_out_f, update_out, row_sums(weight_out_f), row_sums(update_out)
    )
    return (
        new_weight_in,
        new_moment_in,
        new_square_in,
        new_weight_out,
        new_moment_out,
        new_square_out,
    )


def solution(mesh):
    placed = (
        P(("dp", "own"), None, None),
        P(("dp", "own"), None, None),
        P(("dp", "own")),
        P(),
        P("own", None),
        P("own", None),
        P("own", None),
        P("own", None),
        P("own", None),
        P("own", None),
    )
    return jax.shard_map(
        per_device,
        mesh=mesh,
        in_specs=placed,
        out_specs=(
            P("own", None),
            P("own", None),
            P("own", None),
            P("own", None),
            P("own", None),
            P("own", None),
        ),
        check_vma=False,
    )
```

profile of v0, /device:TPU:1, one launch (start us, length us, event | category | flops | bytes accessed | tf_op | source)
XLA Modules:
  0.0 481.7 jit_solution(7212301391568677951)
XLA Ops:
  11.0 2.3 broadcast_select_fusion
  13.3 76.7 %all-gather.3.cloned.1.call-done = bf16[1024,4096]{1,0:T(8,128)(2,1)} async-done(((bf16[64,4096]{1,0:T(8,128)(2,1)}), bf16[1024,4096]{1,0:T(8,128)(2,1)}) %all-gather.3.cloned.1.call-update) | async-done | bytes 8388624 | tf_op jit(solution)/shard_map/all_gather | solution.py:100
  90.0 11.5 %fusion.28 = f32[2,256,4096]{2,1,0:T(8,128)} fusion(bf16[1024,4096]{1,0:T(8,128)(2,1)} %all-gather.3.cloned.1.call-done, bf16[2,256,1024]{2,1,0:T(8,128)(2,1)} %param.12, f32[1024]{0:T(1024)} %param.15, f32[2,256]{1,0:T(2,128)S(1)} %add_rsqrt_fusion), kind=kOutput, calls=%fused_computation.53 | convolution fusion | flops 4297064448 | bytes 17831936 | tf_op jit(solution)/shard_map/dot_general | solution.py:98
  101.6 39.8 %all-gather.5.cloned.1.call-done = bf16[1024,1024]{1,0:T(8,128)(2,1)} async-done(((bf16[64,1024]{1,0:T(8,128)(2,1)}), bf16[1024,1024]{1,0:T(8,128)(2,1)}) %all-gather.5.cloned.1.call-update) | async-done | bytes 2097168 | tf_op jit(solution)/shard_map/all_gather | solution.py:93
  141.3 60.0 %while.13 = (s32[]{:T(128)}, bf16[2,256,4096]{2,1,0:T(8,128)(2,1)}, bf16[2,256,1024]{2,1,0:T(8,128)(2,1)}, f32[2,256,4096]{2,1,0:T(8,128)}, s32[2]{0:T(128)S(1)}...) while((s32[]{:T(128)}, bf16[2,256,4096]{2,1,0:T(8,128)(2,1)}, ...), condition=%wide.region_5.6_spmd.clone, body=%wide.region_2.5_spmd.sunk.clone | while | flops 1372718848 | bytes 94385736 | solution.py:111
  141.3 5.3 %fusion.122 = (bf16[256,4096]{1,0:T(8,128)(2,1)S(1)}, f32[256,4096]{1,0:T(8,128)}) fusion(f32[2,256,4096]{2,1,0:T(8,128)} %get-tuple-element.188, s32[]{:T(128)} %get-tuple-element.178), kind=kLoop, calls=%fused_computation.86.clone.1.clone | loop fusion | flops 5242880 | bytes 10485764 | tf_op jit(solution)/shard_map/convert.8
  151.5 2.3 fusion.133
  153.9 2.5 convolution_convert_fusion.7
  157.1 1.6 fusion.131
  159.2 2.2 fusion.128
  166.4 4.9 %fusion.132 = bf16[2,256,4096]{2,1,0:T(8,128)(2,1)} fusion(bf16[2,256,4096]{2,1,0:T(8,128)(2,1)} %get-tuple-element.179, s32[]{:T(128)} %get-tuple-element.178, f32[2,256,4096]{2,1,0:T(8,128)} %get-tuple-element.188, f32[1,256,1024]{2,1,0:T(8,128)} %copy.90, f32[1,256,1024]{2,1,0:T(8,128)} %copy.91, f32[1,256,1024]{2,1,0:T(8,128)S(1)} %copy.92, ...), kind=kLoop, calls=%fused_computation.10.clone.1.clone | loop fusion | flops 13631488 | bytes 10486272 | tf_op jit(solution)/shard_map/while/body/jit(dynamic_update_index_in_dim)/dynamic_update_slice | solution.py:111
  171.3 5.3 %fusion.122 = (bf16[256,4096]{1,0:T(8,128)(2,1)S(1)}, f32[256,4096]{1,0:T(8,128)}) fusion(f32[2,256,4096]{2,1,0:T(8,128)} %get-tuple-element.188, s32[]{:T(128)} %get-tuple-element.178), kind=kLoop, calls=%fused_computation.86.clone.1.clone | loop fusion | flops 5242880 | bytes 10485764 | tf_op jit(solution)/shard_map/convert.8
  181.5 2.3 fusion.133
  183.8 2.5 convolution_convert_fusion.7
  187.1 1.6 fusion.131
  189.1 2.2 fusion.128
  196.3 5.0 %fusion.132 = bf16[2,256,4096]{2,1,0:T(8,128)(2,1)} fusion(bf16[2,256,4096]{2,1,0:T(8,128)(2,1)} %get-tuple-element.179, s32[]{:T(128)} %get-tuple-element.178, f32[2,256,4096]{2,1,0:T(8,128)} %get-tuple-element.188, f32[1,256,1024]{2,1,0:T(8,128)} %copy.90, f32[1,256,1024]{2,1,0:T(8,128)} %copy.91, f32[1,256,1024]{2,1,0:T(8,128)S(1)} %copy.92, ...), kind=kLoop, calls=%fused_computation.10.clone.1.clone | loop fusion | flops 13631488 | bytes 10486272 | tf_op jit(solution)/shard_map/while/body/jit(dynamic_update_index_in_dim)/dynamic_update_slice | solution.py:111
  201.3 4.3 bitcast_convert_fusion.1
  205.7 9.1 %bitcast_convert_fusion = bf16[1024,4096]{1,0:T(8,128)(2,1)} fusion(bf16[2,256,4096]{2,1,0:T(8,128)(2,1)} %get-tuple-element.44, bf16[2,256,1024]{2,1,0:T(8,128)(2,1)S(1)} %copy-done.12, f32[1024]{0:T(1024)S(1)} %copy-done.18, f32[2,256]{1,0:T(2,128)S(1)} %add_rsqrt_fusion), kind=kOutput, calls=%fused_computation.52 | convolution fusion | flops 4301258752 | bytes 13637632 | tf_op jit(solution)/shard_map/dot_general | solution.py:117
  216.1 67.6 %reduce-scatter.5.cloned.1.call-done = bf16[64,1024]{1,0:T(8,128)(2,1)} async-done(((bf16[1024,1024]{1,0:T(8,128)(2,1)}), bf16[64,1024]{1,0:T(8,128)(2,1)}) %reduce-scatter.5.cloned.1.call-update) | async-done | bytes 131088 | tf_op jit(solution)/shard_map/reduce_scatter | solution.py:123
  283.7 93.7 %reduce-scatter.3.cloned.1.call-done = bf16[64,4096]{1,0:T(8,128)(2,1)} async-done(((bf16[1024,4096]{1,0:T(8,128)(2,1)}), bf16[64,4096]{1,0:T(8,128)(2,1)}) %reduce-scatter.3.cloned.1.call-update) | async-done | bytes 524304 | tf_op jit(solution)/shard_map/reduce_scatter | solution.py:116
  377.4 57.3 %all-reduce.2 = (f32[64,4096]{1,0:T(8,128)S(1)}, f32[64,1024]{1,0:T(8,128)S(1)}) all-reduce(bf16[64,4096]{1,0:T(8,128)(2,1)} %reduce-scatter.3.cloned.1.call-done, bf16[64,1024]{1,0:T(8,128)(2,1)} %reduce-scatter.5.cloned.1.call-done), channel_id=1, replica_groups=mesh['dp'=16,'own'=16] {'dp'}, use_global_device_ids=true, to_apply=%region_7.8 | all-reduce | flops 327680 | bytes 1966080 | tf_op jit(solution)/shard_map/psum | solution.py:126
  437.8 31.5 %psum.23 = f32[]{:T(128)} all-reduce(f32[]{:T(128)S(6)} %add.91), channel_id=1, replica_groups=mesh['dp'=16,'own'=16] {'own'}, use_global_device_ids=true, to_apply=%region_12.13 | all-reduce | flops 1 | bytes 8 | tf_op jit(solution)/shard_map/psum | solution.py:128
  470.3 2.2 multiply_reduce_fusion.1
  (118 shorter events, 31.4 us)
Async XLA Ops:
  7.2 82.9 %all-gather.3.cloned.1.call-start = ((), (), s32[]{:S(2)}) async-start(), calls=%async_computation.2 | async-start | bytes 8912896 | tf_op jit(solution)/shard_map/all_gather | solution.py:100
  7.9 133.4 %all-gather.5.cloned.1.call-start = ((), (), s32[]{:S(2)}) async-start(), calls=%async_computation.3 | async-start | bytes 2228224 | tf_op jit(solution)/shard_map/all_gather | solution.py:93
  8.6 275.1 %reduce-scatter.5.cloned.1.call-start = ((), (), s32[]{:S(2)}) async-start(), calls=%async_computation.5 | async-start | bytes 2228224 | tf_op jit(solution)/shard_map/reduce_scatter | solution.py:123
  13.3 128.0 %copy-start.19 = (s32[2]{0:T(128)S(1)}, s32[2]{0:T(128)}, u32[]{:S(2)}) copy-start(s32[2]{0:T(128)} %param.14) | copy-start | bytes 28
  147.0 3.4 copy-start.1
  147.2 3.2 copy-start.2
  150.2 6.2 %copy-start.5 = (bf16[4,256,256]{2,1,0:T(8,128)(2,1)}, bf16[4,256,256]{2,1,0:T(8,128)(2,1)S(1)}, u32[]{:S(2)}) copy-start(bf16[4,256,256]{2,1,0:T(8,128)(2,1)S(1)} %get-tuple-element.157) | copy-start | bytes 1572868 | tf_op jit(solution)/shard_map/while
  151.5 4.9 %copy-start = (f32[256,4096]{1,0:T(8,128)S(1)}, f32[256,4096]{1,0:T(8,128)}, u32[]{:S(2)}) copy-start(f32[256,4096]{1,0:T(8,128)} %get-tuple-element.159) | copy-start | bytes 12582916 | tf_op jit(solution)/shard_map/while
  159.1 2.3 copy-start.3
  177.0 3.4 copy-start.1
  177.2 3.2 copy-start.2
  180.2 6.2 %copy-start.5 = (bf16[4,256,256]{2,1,0:T(8,128)(2,1)}, bf16[4,256,256]{2,1,0:T(8,128)(2,1)S(1)}, u32[]{:S(2)}) copy-start(bf16[4,256,256]{2,1,0:T(8,128)(2,1)S(1)} %get-tuple-element.157) | copy-start | bytes 1572868 | tf_op jit(solution)/shard_map/while
  181.5 4.9 %copy-start = (f32[256,4096]{1,0:T(8,128)S(1)}, f32[256,4096]{1,0:T(8,128)}, u32[]{:S(2)}) copy-start(f32[256,4096]{1,0:T(8,128)} %get-tuple-element.159) | copy-start | bytes 12582916 | tf_op jit(solution)/shard_map/while
  201.3 4.4 copy-start.12
  201.3 4.4 copy-start.18
  205.6 171.8 %reduce-scatter.3.cloned.1.call-start = ((), (), s32[]{:S(2)}) async-start(), calls=%async_computation.4 | async-start | bytes 8912896 | tf_op jit(solution)/shard_map/reduce_scatter | solution.py:116
  214.8 222.8 %copy-start.11 = (bf16[64,1024]{1,0:T(8,128)(2,1)S(1)}, bf16[64,1024]{1,0:T(8,128)(2,1)}, u32[]{:S(2)}) copy-start(bf16[64,1024]{1,0:T(8,128)(2,1)} %param.17) | copy-start | bytes 393220
  214.8 255.1 %copy-start.16 = (f32[64,1024]{1,0:T(8,128)S(1)}, f32[64,1024]{1,0:T(8,128)}, u32[]{:S(2)}) copy-start(f32[64,1024]{1,0:T(8,128)} %param.20) | copy-start | bytes 786436
  214.8 255.1 %copy-start.17 = (f32[64,1024]{1,0:T(8,128)S(1)}, f32[64,1024]{1,0:T(8,128)}, u32[]{:S(2)}) copy-start(f32[64,1024]{1,0:T(8,128)} %param.21) | copy-start | bytes 786436
  214.9 255.5 %copy-start.15 = (f32[64,4096]{1,0:T(8,128)S(1)}, f32[64,4096]{1,0:T(8,128)}, u32[]{:S(2)}) copy-start(f32[64,4096]{1,0:T(8,128)} %param.18) | copy-start | bytes 3145732
  470.3 4.9 %copy-start.13 = (f32[64,1024]{1,0:T(8,128)}, f32[64,1024]{1,0:T(8,128)S(1)}, u32[]{:S(2)}) copy-start(f32[64,1024]{1,0:T(8,128)S(1)} %get-tuple-element.65) | copy-start | bytes 786436
  470.3 4.9 %copy-start.14 = (f32[64,1024]{1,0:T(8,128)}, f32[64,1024]{1,0:T(8,128)S(1)}, u32[]{:S(2)}) copy-start(f32[64,1024]{1,0:T(8,128)S(1)} %get-tuple-element.66) | copy-start | bytes 786436
  472.6 2.6 copy-start.9
  472.6 2.6 copy-start.10
  (8 other events, 9.7 us)
Sparse Core Ops, SparseCore 0:
  10.4 79.5 all-gather.2
  92.5 48.8 all-gather.4
  205.7 77.9 reduce-scatter.4
  287.7 89.6 reduce-scatter.2
where the time goes:
time: 490 us; the launch traced here: 482 us
  waiting for transfers between devices  279 us (57%)
  blocking collectives  88.8 us (18%)
  matrix products  45 us (9%)
  other arithmetic  39.8 us (8%)
  between operations  16 us (3%)
  local copies, waits for them, and re-layouts  12.3 us (3%)
    reduce_scatter x1, waiting for transfers between devices, per_device(): lax.psum_scatter(jnp.dot(columns.T, grad_rows, preferred_element_type=jnp...  93.7 us
    all_gather x1, waiting for transfers between devices, per_device(): lax.all_gather(weight_in, 'own', axis=0, tiled=True)  76.7 us
    reduce_scatter x1, waiting for transfers between devices, per_device(): lax.psum_scatter(term_out.astype(jnp.bfloat16), 'own', scatter_dimension=...  67.6 us
    psum x1, blocking collectives, per_device(): grad_in, grad_out = lax.psum((part_in, part_out), 'dp')  57.3 us
    all_gather x1, waiting for transfers between devices, per_device(): weight_full = lax.all_gather(weight_out, 'own', axis=0, tiled=True)  39.8 us
    psum x1, blocking collectives, per_device(): square_total = lax.psum(local_square, 'own')  31.5 us
    dynamic_update_slice x4, other arithmetic, per_device(): grad_projected, gated = lax.map(one_slot, (projected, cot_masked, lengths))  14.6 us
    dot_general x1, matrix products, per_device(): jnp.dot(columns, lax.all_gather(weight_in, 'own', axis=0, tiled=True), pr...  11.5 us
  transfers between devices with their start and end apart: 4, of which 4 were waited for; matrix products, arithmetic and copies ran while one was open for 5% of the time, Pallas kernels for 0%

commit v1 on v0

v1 whole, which is shorter than its diff:
```python
import jax
import jax.numpy as jnp
from jax import lax
from jax.experimental import pallas as pl
from jax.experimental.pallas import tpu as pltpu
from jax.sharding import Mesh
from jax.sharding import PartitionSpec as P

BLK = 256
HEAD_WIDTH = 256

norm_eps = 1e-06
beta_first = 0.9
beta_second = 0.95
learn_rate = 0.01
step_number = 10.0
update_eps = 1e-08
ratio_eps = 1e-06

OWN = ("x", "y")
SWAP = ((0, 1), (1, 0))


def rms_scale(values):
    return values * lax.rsqrt(jnp.mean(values * values, axis=-1, keepdims=True) + norm_eps)


def sigmoid(values):
    return 1.0 / (1.0 + jnp.exp(-values))


def allowed_mask(length):
    row = lax.broadcasted_iota(jnp.int32, (BLK, BLK), 0)
    col = lax.broadcasted_iota(jnp.int32, (BLK, BLK), 1)
    return ((col <= row) & (row < length)).astype(jnp.float32) * (1.0 / BLK)


def dot_nt(left, right):
    return lax.dot_general(
        left, right, (((1,), (1,)), ((), ())), preferred_element_type=jnp.float32
    )


def dot_tn(left, right):
    return lax.dot_general(
        left, right, (((0,), (0,)), ((), ())), preferred_element_type=jnp.float32
    )


def forward_kernel(lengths, normed, weight, projected, scores, mixed):
    width = weight.shape[1] // 4
    proj = jnp.dot(normed[0], weight[...], preferred_element_type=jnp.float32)
    projected[0] = proj
    rest = proj[:, width:]
    rest = (rest * sigmoid(rest)).astype(jnp.bfloat16)
    allowed = allowed_mask(lengths[pl.program_id(0)])
    for head in range(width // HEAD_WIDTH):
        start = head * HEAD_WIDTH
        values = rest[:, start : start + HEAD_WIDTH]
        queries = rest[:, width + start : width + start + HEAD_WIDTH]
        key_part = rest[:, 2 * width + start : 2 * width + start + HEAD_WIDTH]
        score = dot_nt(queries, key_part) * HEAD_WIDTH ** (-0.5)
        scores[0, head] = score
        attention = (score * sigmoid(score) * allowed).astype(jnp.bfloat16)
        mixed[0, :, start : start + HEAD_WIDTH] = jnp.dot(
            attention, values, preferred_element_type=jnp.float32
        )


def stats_kernel(masked, weight_out, projected, mixed, grad_gated, stats):
    grad = dot_nt(masked[0], weight_out[...]).astype(jnp.bfloat16)
    grad_gated[0] = grad
    proj = projected[0]
    mix = mixed[0]
    square = jnp.sum(mix * mix, axis=1, keepdims=True)
    cross = jnp.sum(
        grad.astype(jnp.float32) * (proj * sigmoid(proj)) * mix, axis=1, keepdims=True
    )
    lane = lax.broadcasted_iota(jnp.int32, (BLK, 128), 1)
    stats[0] = jnp.where(lane == 0, square, cross)


def backward_kernel(
    lengths, projected, scores, mixed, grad_gated, stats, stats_other, gated, grad_proj
):
    width = mixed.shape[2]
    model_width = 2 * width
    total = stats[0] + stats_other[0]
    inv = lax.rsqrt(total[:, 0:1] / model_width + norm_eps)
    back = inv * inv * inv * (total[:, 1:2] / model_width)
    allowed = allowed_mask(lengths[pl.program_id(0)])

    proj = projected[0, :, :width]
    sig = sigmoid(proj)
    gating = proj * sig
    mix = mixed[0]
    grad = grad_gated[0].astype(jnp.float32)
    scaled = mix * inv
    gated[0] = (scaled * gating).astype(jnp.bfloat16)
    grad_proj[0, :, :width] = (grad * scaled * (sig + gating * (1.0 - sig))).astype(jnp.bfloat16)
    grad_mixed = (inv * (grad * gating) - mix * back).astype(jnp.bfloat16)

    for head in range(width // HEAD_WIDTH):
        start = head * HEAD_WIDTH
        acts, slopes = [], []
        for part in (1, 2, 3):
            block = projected[0, :, part * width + start : part * width + start + HEAD_WIDTH]
            sig = sigmoid(block)
            act = block * sig
            acts.append(act.astype(jnp.bfloat16))
            slopes.append(sig + act * (1.0 - sig))
        values, queries, key_part = acts
        score = scores[0, head]
        sig = sigmoid(score)
        act = score * sig
        attention = (act * allowed).astype(jnp.bfloat16)
        grad_head = grad_mixed[:, start : start + HEAD_WIDTH]
        grad_att = dot_nt(grad_head, values).astype(jnp.bfloat16).astype(jnp.float32)
        grad_score = (
            grad_att * allowed * (sig + act * (1.0 - sig)) * HEAD_WIDTH ** (-0.5)
        ).astype(jnp.bfloat16)
        grads = (
            dot_tn(attention, grad_head),
            jnp.dot(grad_score, key_part, preferred_element_type=jnp.float32),
            dot_tn(grad_score, queries),
        )
        for part in (1, 2, 3):
            held = grads[part - 1].astype(jnp.bfloat16).astype(jnp.float32)
            grad_proj[0, :, part * width + start : part * width + start + HEAD_WIDTH] = (
                held * slopes[part - 1]
            ).astype(jnp.bfloat16)


def row_block(*dims):
    return pl.BlockSpec((1, *dims), lambda i, *_: (i,) + (0,) * len(dims))


def whole_block(*dims):
    return pl.BlockSpec(dims, lambda i, *_: (0,) * len(dims))


VMEM_LIMIT = 48 * 1024 * 1024


def attention_forward(lengths, normed, weight):
    count, rows, depth = normed.shape
    columns = weight.shape[1]
    width = columns // 4
    heads = width // HEAD_WIDTH
    return pl.pallas_call(
        forward_kernel,
        grid_spec=pltpu.PrefetchScalarGridSpec(
            num_scalar_prefetch=1,
            grid=(count,),
            in_specs=[row_block(rows, depth), whole_block(depth, columns)],
            out_specs=[
                row_block(rows, columns),
                row_block(heads, rows, rows),
                row_block(rows, width),
            ],
        ),
        out_shape=[
            jax.ShapeDtypeStruct((count, rows, columns), jnp.float32),
            jax.ShapeDtypeStruct((count, heads, rows, rows), jnp.float32),
            jax.ShapeDtypeStruct((count, rows, width), jnp.float32),
        ],
        compiler_params=pltpu.CompilerParams(vmem_limit_bytes=VMEM_LIMIT),
        name="attention_forward",
    )(lengths, normed, weight)


def norm_stats(masked, weight_out, projected, mixed):
    count, rows, model_width = masked.shape
    width = weight_out.shape[0]
    return pl.pallas_call(
        stats_kernel,
        grid=(count,),
        in_specs=[
            row_block(rows, model_width),
            whole_block(width, model_width),
            row_block(rows, width),
            row_block(rows, width),
        ],
        out_specs=[row_block(rows, width), row_block(rows, 128)],
        out_shape=[
            jax.ShapeDtypeStruct((count, rows, width), jnp.bfloat16),
            jax.ShapeDtypeStruct((count, rows, 128), jnp.float32),
        ],
        compiler_params=pltpu.CompilerParams(vmem_limit_bytes=VMEM_LIMIT),
        name="norm_stats",
    )(masked, weight_out, projected, mixed)


def attention_backward(lengths, projected, scores, mixed, grad_gated, stats, stats_other):
    count, rows, columns = projected.shape
    width = columns // 4
    heads = width // HEAD_WIDTH
    return pl.pallas_call(
        backward_kernel,
        grid_spec=pltpu.PrefetchScalarGridSpec(
            num_scalar_prefetch=1,
            grid=(count,),
            in_specs=[
                row_block(rows, columns),
                row_block(heads, rows, rows),
                row_block(rows, width),
                row_block(rows, width),
                row_block(rows, 128),
                pl.BlockSpec((1, rows, 128), lambda i, *_: ((i + count // 2) % count, 0, 0)),
            ],
            out_specs=[row_block(rows, width), row_block(rows, columns)],
        ),
        out_shape=[
            jax.ShapeDtypeStruct((count, rows, width), jnp.bfloat16),
            jax.ShapeDtypeStruct((count, rows, columns), jnp.bfloat16),
        ],
        compiler_params=pltpu.CompilerParams(vmem_limit_bytes=VMEM_LIMIT),
        name="attention_backward",
    )(lengths, projected, scores, mixed, grad_gated, stats, stats_other)


def adam_parts(gradient, moment, square, clip_factor):
    scaled = gradient * clip_factor
    new_moment = beta_first * moment + (1.0 - beta_first) * scaled
    new_square = beta_second * square + (1.0 - beta_second) * scaled * scaled
    update = (
        new_moment
        / (1.0 - beta_first**step_number)
        / (jnp.sqrt(new_square / (1.0 - beta_second**step_number)) + update_eps)
    )
    return (new_moment, new_square, update)


def trust_step(weight, update):
    weight = weight.astype(jnp.float32)
    weight_sq = jnp.sum(weight * weight, axis=1, keepdims=True)
    update_sq = jnp.sum(update * update, axis=1, keepdims=True)
    trust_ratio = jnp.sqrt(weight_sq) / (jnp.sqrt(update_sq) + ratio_eps)
    return weight - learn_rate * trust_ratio * update


def swap_cores(values):
    return lax.ppermute(values, "c", SWAP)


def in_core_order(core, mine, other, axis):
    first = jnp.where(core == 0, mine, other)
    second = jnp.where(core == 0, other, mine)
    return jnp.stack([first, second], axis=axis)


def exchange(blocks, axes):
    return lax.all_to_all(blocks, axes, 0, 0, tiled=True)


def per_device(
    tokens,
    cotangent,
    lengths,
    norm_gain,
    weight_in,
    weight_out,
    moment_in,
    square_in,
    moment_out,
    square_out,
):
    slots, rows, model_width = tokens.shape
    half = model_width // 2
    core = lax.axis_index("c")
    owners = lax.axis_size(OWN)
    planes = lax.axis_size("z")
    owned = weight_in.shape[0]

    weight_out_full = lax.all_gather(weight_out, OWN, axis=0, tiled=True)
    mine = lax.dynamic_index_in_dim(
        weight_in.reshape(owned, 4, 2, half), core, axis=2, keepdims=False
    ).reshape(owned, 4 * half)
    weight_cols = exchange(
        jnp.broadcast_to(mine[None], (owners, *mine.shape)).reshape(owners * owned, -1), OWN
    )

    normed = (rms_scale(tokens.astype(jnp.float32)) * norm_gain).astype(jnp.bfloat16)
    row_index = jnp.arange(rows, dtype=jnp.int32)
    live = row_index[None, :] < lengths[:, None]
    masked = jnp.where(live[:, :, None], cotangent, jnp.zeros_like(cotangent))
    normed = jnp.concatenate([normed, swap_cores(normed)], axis=0)
    masked = jnp.concatenate([masked, swap_cores(masked)], axis=0)
    lengths = jnp.concatenate([lengths, swap_cores(lengths)], axis=0)

    projected, scores, mixed = attention_forward(lengths, normed, weight_cols)
    weight_rows = lax.dynamic_slice_in_dim(weight_out_full, core * half, half, axis=0)
    grad_gated, stats = norm_stats(masked, weight_rows, projected, mixed)
    gated, grad_proj = attention_backward(
        lengths, projected, scores, mixed, grad_gated, stats, swap_cores(stats)
    )

    normed_rows = normed.reshape(-1, model_width)
    masked_rows = masked.reshape(-1, model_width)
    term_in = dot_tn(normed_rows, grad_proj.reshape(normed_rows.shape[0], -1)).astype(jnp.bfloat16)
    term_out = dot_tn(gated.reshape(-1, half), masked_rows).astype(jnp.bfloat16)
    columns = term_out.reshape(half, 2, half)
    keep = lax.dynamic_index_in_dim(columns, core, axis=1, keepdims=False)
    give = lax.dynamic_index_in_dim(columns, 1 - core, axis=1, keepdims=False)
    term_out = in_core_order(core, keep, swap_cores(give), 0).reshape(model_width, half)

    term = jnp.concatenate([term_in, term_out], axis=1)
    part = jnp.sum(
        exchange(term, OWN).reshape(owners, owned, -1).astype(jnp.float32), axis=0
    ).astype(jnp.bfloat16)
    piece = jnp.sum(
        exchange(part, "z").reshape(planes, owned // planes, -1).astype(jnp.float32), axis=0
    ).astype(jnp.bfloat16)
    shard = exchange(
        jnp.broadcast_to(piece[None], (planes, *piece.shape)).reshape(owned, -1), "z"
    )
    grad = in_core_order(core, shard.reshape(owned, 5, half), swap_cores(shard).reshape(owned, 5, half), 2)
    grad = grad.astype(jnp.float32)
    grad_in = grad[:, :4].reshape(owned, 4 * model_width)
    grad_out = grad[:, 4].reshape(owned, model_width)

    local_square = jnp.sum(grad * grad)
    squares = exchange(jnp.broadcast_to(local_square, (owners, 8, 128)).reshape(-1, 128), OWN)
    square_total = jnp.sum(squares.reshape(owners, 8, 128)[:, 0, 0])
    clip_factor = jnp.minimum(
        1.0, jnp.sqrt(5.0 * model_width * model_width / (square_total + norm_eps))
    )
    new_moment_in, new_square_in, update_in = adam_parts(grad_in, moment_in, square_in, clip_factor)
    new_moment_out, new_square_out, update_out = adam_parts(
        grad_out, moment_out, square_out, clip_factor
    )
    return (
        trust_step(weight_in, update_in),
        new_moment_in,
        new_square_in,
        trust_step(weight_out, update_out),
        new_moment_out,
        new_square_out,
    )


def solution(mesh):
    fine = Mesh(mesh.devices.reshape(8, 2, 4, 4), ("z", "c", "x", "y"))
    histories = ("z", "c", "x", "y")
    placed = (
        P(histories, None, None),
        P(histories, None, None),
        P(histories),
        P(),
        P(OWN, None),
        P(OWN, None),
        P(OWN, None),
        P(OWN, None),
        P(OWN, None),
        P(OWN, None),
    )
    return jax.shard_map(
        per_device,
        mesh=fine,
        in_specs=placed,
        out_specs=(P(OWN, None),) * 6,
        check_vma=False,
    )
```

time: 490 us -> 278 us (0.57); the launches traced: 482 us -> 277 us
  waiting for transfers between devices: 279 us -> 75.7 us
  matrix products: 45 us -> 8.61 us
  Pallas kernels: 0 us -> 26 us
  other arithmetic: 39.8 us -> 17 us
  starting transfers between devices: 0.16 us -> 21 us
  blocking collectives: 88.8 us -> 95.3 us
  local copies, waits for them, and re-layouts: 12.3 us -> 18.3 us
    reduce_scatter x2 -> x0, waiting for transfers between devices: 161 us -> none  [the longest x1 93.7 us: per_device(): lax.psum_scatter(jnp.dot(columns.T, grad_rows, preferred_element_type=jnp...]
    all_gather x2 -> x1, waiting for transfers between devices: 116 us -> 11.4 us  [per_device(): weight_out_full = lax.all_gather(weight_out, OWN, axis=0, tiled=True)]
    all_to_all x0 -> x3, blocking collectives: none -> 95.3 us  [exchange(): return lax.all_to_all(blocks, axes, 0, 0, tiled=True)]
    psum x2 -> x0, blocking collectives: 88.8 us -> none  [the longest x1 57.3 us: per_device(): grad_in, grad_out = lax.psum((part_in, part_out), 'dp')]
    all_to_all x0 -> x2, waiting for transfers between devices: none -> 59.6 us  [exchange(): return lax.all_to_all(blocks, axes, 0, 0, tiled=True)]
    dot_general x17 -> x2, matrix products: 45 us -> 8.61 us  [dot_tn(): lax.dot_general(left, right, (((0,), (0,)), ((), ())), preferred_element_...]
    pallas_call x0 -> x3, Pallas kernels: none -> 26 us  [the longest x1 11 us: attention_forward(): pl.pallas_call(forward_kernel, grid_spec=pltpu.PrefetchScalarGridSpec(num...]
    dynamic_update_slice x4 -> x0, other arithmetic: 14.6 us -> none  [per_device(): grad_projected, gated = lax.map(one_slot, (projected, cot_masked, lengths))]
  transfers between devices with their start and end apart: 4 -> 9, of which waited for: 4 -> 7; matrix products, arithmetic and copies ran while one was open for 5% -> 4% of each run, Pallas kernels for 0% -> 4%
where the time goes in v1:
time: 278 us; the launch traced here: 277 us
  blocking collectives  95.3 us (34%)
  waiting for transfers between devices  75.7 us (27%)
  Pallas kernels  26 us (9%)
  starting transfers between devices  21 us (8%)
  local copies, waits for them, and re-layouts  18.3 us (7%)
  other arithmetic  17 us (6%)
  between operations  15.2 us (5%)
  matrix products  8.61 us (3%)
    all_to_all x3, blocking collectives, exchange(): return lax.all_to_all(blocks, axes, 0, 0, tiled=True)  95.3 us
    all_to_all x2, waiting for transfers between devices, exchange(): return lax.all_to_all(blocks, axes, 0, 0, tiled=True)  59.6 us
    all_to_all x2, starting transfers between devices, exchange(): return lax.all_to_all(blocks, axes, 0, 0, tiled=True)  12.7 us
    all_gather x1, waiting for transfers between devices, per_device(): weight_out_full = lax.all_gather(weight_out, OWN, axis=0, tiled=True)  11.4 us
    pallas_call x1, Pallas kernels, attention_forward(): pl.pallas_call(forward_kernel, grid_spec=pltpu.PrefetchScalarGridSpec(num...  11 us
    pallas_call x1, Pallas kernels, attention_backward(): pl.pallas_call(backward_kernel, grid_spec=pltpu.PrefetchScalarGridSpec(nu...  9.86 us
    dot_general x2, matrix products, dot_tn(): lax.dot_general(left, right, (((0,), (0,)), ((), ())), preferred_element_...  8.61 us
    ppermute x6, starting transfers between devices, swap_cores(): return lax.ppermute(values, 'c', SWAP)  8.29 us
  transfers between devices with their start and end apart: 9, of which 7 were waited for; matrix products, arithmetic and copies ran while one was open for 4% of the time, Pallas kernels for 4%

profile of v1, /device:TPU:1, one launch (start us, length us, event | category | flops | bytes accessed | tf_op | source)
XLA Modules:
  0.0 277.1 jit_solution(14224785901328417546)
XLA Ops:
  8.6 1.6 dynamic-slice_reduce_fusion
  10.3 2.5 broadcast_in_dim.17
  12.8 7.8 %all-to-all-start = ((bf16[16,64,2048]{2,1,0:T(8,128)(2,1)}), bf16[16,64,2048]{2,1,0:T(8,128)(2,1)}, u32[]{:S(2)}, u32[]{:S(2)}) async-start(bf16[16,64,2048]{2,1,0:T(8,128)(2,1)} %broadcast_in_dim.17), calls=%async_computation | async-start | bytes 8388608 | tf_op jit(solution)/shard_map/all_to_all | solution.py:253
  25.4 2.7 pad_maximum_fusion.1.normed
  28.1 1.7 pad_maximum_fusion.2.masked
  29.9 53.2 %all-to-all-done = bf16[16,64,2048]{2,1,0:T(8,128)(2,1)} async-done(((bf16[16,64,2048]{2,1,0:T(8,128)(2,1)}), bf16[16,64,2048]{2,1,0:T(8,128)(2,1)}, u32[]{:S(2)}, u32[]{:S(2)}) %all-to-all-start) | async-done | bytes 4194336 | tf_op jit(solution)/shard_map/all_to_all | solution.py:253
  83.1 11.0 %attention_forward.1 = (f32[4,256,2048]{2,1,0:T(8,128)}, f32[4,2,256,256]{3,2,1,0:T(8,128)S(1)}, f32[4,256,512]{2,1,0:T(8,128)S(1)}) custom-call(s32[4]{0:T(128)S(1)} %pad_add_fusion.lengths, bf16[4,256,1024]{2,1,0:T(8,128)(2,1)} %pad_maximum_fusion.1.normed, bf16[1024,2048]{1,0:T(8,128)(2,1)} %bitcast.weight), custom_call_target="tpu_custom_call" | custom-call | tf_op jit(solution)/shard_map/attention_forward/pallas_call | solution.py:150
  96.8 11.4 %all-gather.2.cloned.1.call-done = bf16[1024,1024]{1,0:T(8,128)(2,1)} async-done(((bf16[64,1024]{1,0:T(8,128)(2,1)}), bf16[1024,1024]{1,0:T(8,128)(2,1)}) %all-gather.2.cloned.1.call-update) | async-done | bytes 2097168 | tf_op jit(solution)/shard_map/all_gather | solution.py:275
  109.4 5.1 %norm_stats.1 = (bf16[4,256,512]{2,1,0:T(8,128)(2,1)S(1)}, f32[4,256,128]{2,1,0:T(8,128)}) custom-call(bf16[4,256,1024]{2,1,0:T(8,128)(2,1)S(1)} %pad_maximum_fusion.2.masked, bf16[512,1024]{1,0:T(8,128)(2,1)S(1)} %constant_dynamic-slice_fusion.2.weight_out, f32[4,256,2048]{2,1,0:T(8,128)} %get-tuple-element.13.projected, f32[4,256,512]{2,1,0:T(8,128)} %copy-done), custom_call_target="tpu_custom_call" | custom-call | tf_op jit(solution)/shard_map/norm_stats/pallas_call | solution.py:175
  116.0 1.7 collective-permute-done.3.stats_other
  117.8 1.6 copy-done.2
  119.4 9.9 %attention_backward.1 = (bf16[4,256,512]{2,1,0:T(8,128)(2,1)S(1)}, bf16[4,256,2048]{2,1,0:T(8,128)(2,1)}) custom-call(s32[4]{0:T(128)S(1)} %pad_add_fusion.lengths, f32[4,256,2048]{2,1,0:T(8,128)} %get-tuple-element.13.projected, f32[4,2,256,256]{3,2,1,0:T(8,128)S(1)} %copy-done.2, f32[4,256,512]{2,1,0:T(8,128)} %copy-done, ...), custom_call_target="tpu_custom_call" | custom-call | tf_op jit(solution)/shard_map/attention_backward/pallas_call | solution.py:198
  129.3 2.5 bitcast_convert_fusion.1
  132.6 2.2 constant_dynamic-slice_fusion.1
  135.4 6.1 %bitcast_convert_fusion = bf16[1024,2048]{1,0:T(8,128)(2,1)S(1)} fusion(bf16[4,256,2048]{2,1,0:T(8,128)(2,1)S(1)} %copy-done.18, bf16[2,256,1024]{2,1,0:T(8,128)(2,1)} %collective-permute-done, bf16[2,256,1024]{2,1,0:T(8,128)(2,1)S(1)} %copy-done.6), kind=kOutput, calls=%fused_computation | convolution fusion | flops 4298113024 | bytes 10485760 | tf_op jit(solution)/shard_map/dot_general | solution.py:45
  142.2 65.3 %all_to_all.38 = bf16[16,64,2560]{2,1,0:T(8,128)(2,1)} all-to-all(bf16[16,64,2560]{2,1,0:T(8,128)(2,1)S(1)} %pad_maximum_fusion), channel_id=1, replica_groups=mesh['z'=8,'c'=2,'x'=4,'y'=4] {'x','y'}, dimensions={0} | all-to-all | bytes 10485760 | tf_op jit(solution)/shard_map/all_to_all | solution.py:253
  207.4 3.2 %reduce_sum.89 = bf16[64,2560]{1,0:T(8,128)(2,1)S(1)} reduce(bf16[16,64,2560]{2,1,0:T(8,128)(2,1)} %all_to_all.38, bf16[]{:T(256)} %constant.30.clone.1), dimensions={0}, to_apply=%region_2.3 | reduce | flops 2457600 | bytes 5570562 | tf_op jit(solution)/shard_map/reduce_sum | solution.py:308
  210.7 16.8 %all_to_all.39 = bf16[8,8,2560]{2,1,0:T(8,128)(2,1)S(1)} all-to-all(bf16[8,8,2560]{2,1,0:T(8,128)(2,1)S(1)} %bitcast.32), channel_id=1, replica_groups=mesh['z'=8,'c'=2,'x'=4,'y'=4] {'z'}, dimensions={0} | all-to-all | bytes 655360 | tf_op jit(solution)/shard_map/all_to_all | solution.py:253
  227.6 13.2 %all_to_all.40 = bf16[8,8,2560]{2,1,0:T(8,128)(2,1)S(1)} all-to-all(bf16[8,8,2560]{2,1,0:T(8,128)(2,1)S(1)} %broadcast_in_dim.20), channel_id=1, replica_groups=mesh['z'=8,'c'=2,'x'=4,'y'=4] {'z'}, dimensions={0} | all-to-all | bytes 655360 | tf_op jit(solution)/shard_map/all_to_all | solution.py:253
  240.8 4.7 %collective-permute-start.5 = (bf16[64,2560]{1,0:T(8,128)(2,1)S(1)}, bf16[64,2560]{1,0:T(8,128)(2,1)S(1)}, u32[]{:S(2)}, u32[]{:S(2)}) collective-permute-start(bf16[64,2560]{1,0:T(8,128)(2,1)S(1)} %bitcast.33), channel_id=1, source_target_pairs={{0,16},{16,0},{1,17},{17,1},{2,18},{18,2},{3,19},{19,3},{4,20},{20... | collective-permute-start | bytes 983048 | tf_op jit(solution)/shard_map/ppermute | solution.py:243
  249.7 4.9 %all-to-all-start.4 = ((f32[16,8,128]{2,1,0:T(8,128)}), f32[16,8,128]{2,1,0:T(8,128)S(1)}, u32[]{:S(2)}, u32[]{:S(2)}) async-start(f32[16,8,128]{2,1,0:T(8,128)} %reshape.161), calls=%async_computation.4 | async-start | bytes 131072 | tf_op jit(solution)/shard_map/all_to_all | solution.py:253
  254.7 6.4 %all-to-all-done.4 = f32[16,8,128]{2,1,0:T(8,128)S(1)} async-done(((f32[16,8,128]{2,1,0:T(8,128)}), f32[16,8,128]{2,1,0:T(8,128)S(1)}, u32[]{:S(2)}, u32[]{:S(2)}) %all-to-all-start.4) | async-done | bytes 65568 | tf_op jit(solution)/shard_map/all_to_all | solution.py:253
  265.0 2.6 multiply_reduce_fusion.1
  268.8 1.5 convert_subtract_fusion
  (85 shorter events, 22.3 us)
Async XLA Ops:
  12.8 8.5 %copy-start.4 = (bf16[2,256,1024]{2,1,0:T(8,128)(2,1)S(1)}, bf16[2,256,1024]{2,1,0:T(8,128)(2,1)}, u32[]{:S(2)}) copy-start(bf16[2,256,1024]{2,1,0:T(8,128)(2,1)} %param.10) | copy-start | bytes 3145732
  12.8 8.8 %copy-start.17 = (f32[1024]{0:T(1024)S(1)}, f32[1024]{0:T(1024)}, u32[]{:S(2)}) copy-start(f32[1024]{0:T(1024)} %param.13) | copy-start | bytes 12292
  12.8 70.3 %all-to-all-start = ((bf16[16,64,2048]{2,1,0:T(8,128)(2,1)}), bf16[16,64,2048]{2,1,0:T(8,128)(2,1)}, u32[]{:S(2)}, u32[]{:S(2)}) async-start(bf16[16,64,2048]{2,1,0:T(8,128)(2,1)} %broadcast_in_dim.17), calls=%async_computation | async-start | bytes 8388608 | tf_op jit(solution)/shard_map/all_to_all | solution.py:253
  20.6 2.4 copy-start.19
  20.6 2.5 copy-start.14
  20.6 87.6 %all-gather.2.cloned.1.call-start = ((), (), s32[]{:S(2)}) async-start(), calls=%async_computation.5 | async-start | bytes 2228224 | tf_op jit(solution)/shard_map/all_gather | solution.py:275
  21.9 6.2 %copy-start.5 = (bf16[2,256,1024]{2,1,0:T(8,128)(2,1)}, bf16[2,256,1024]{2,1,0:T(8,128)(2,1)S(1)}, u32[]{:S(2)}) copy-start(bf16[2,256,1024]{2,1,0:T(8,128)(2,1)S(1)} %fusion.2) | copy-start | bytes 3145732
  21.9 3.5 %collective-permute-start = (bf16[2,256,1024]{2,1,0:T(8,128)(2,1)S(1)}, bf16[2,256,1024]{2,1,0:T(8,128)(2,1)}, u32[]{:S(2)}, u32[]{:S(2)}) collective-permute-start(bf16[2,256,1024]{2,1,0:T(8,128)(2,1)S(1)} %fusion.2), channel_id=1, source_target_pairs={{0,16},{16,0},{1,17},{17,1},{2,18},{18,2},{3,19},{19,3},{4,20},{20... | collective-permute-start | bytes 3145736 | tf_op jit(solution)/shard_map/ppermute | solution.py:243
  23.2 4.9 %copy-start.7 = (bf16[2,256,1024]{2,1,0:T(8,128)(2,1)}, bf16[2,256,1024]{2,1,0:T(8,128)(2,1)S(1)}, u32[]{:S(2)}) copy-start(bf16[2,256,1024]{2,1,0:T(8,128)(2,1)S(1)} %broadcast_select_fusion) | copy-start | bytes 3145732
  23.2 4.9 %collective-permute-start.2 = (bf16[2,256,1024]{2,1,0:T(8,128)(2,1)S(1)}, bf16[2,256,1024]{2,1,0:T(8,128)(2,1)}, u32[]{:S(2)}, u32[]{:S(2)}) collective-permute-start(bf16[2,256,1024]{2,1,0:T(8,128)(2,1)S(1)} %broadcast_select_fusion), channel_id=1, source_target_pairs={{0,16},{16,0},{1,17},{17,1},{2,18},{18,2},{3,19},{19,3},{4,20},{20... | collective-permute-start | bytes 3145736 | tf_op jit(solution)/shard_map/ppermute | solution.py:243
  23.3 1.9 collective-permute-start.1
  114.5 3.2 %collective-permute-start.3 = (f32[4,256,128]{2,1,0:T(8,128)}, f32[4,256,128]{2,1,0:T(8,128)S(1)}, u32[]{:S(2)}, u32[]{:S(2)}) collective-permute-start(f32[4,256,128]{2,1,0:T(8,128)} %get-tuple-element.17.stats), channel_id=1, source_target_pairs={{0,16},{16,0},{1,17},{17,1},{2,18},{18,2},{3,19},{19,3},{4,20},{20... | collective-permute-start | bytes 1572872 | tf_op jit(solution)/shard_map/ppermute | solution.py:243
  119.4 9.9 %copy-start.8 = (bf16[2,256,1024]{2,1,0:T(8,128)(2,1)S(1)}, bf16[2,256,1024]{2,1,0:T(8,128)(2,1)}, u32[]{:S(2)}) copy-start(bf16[2,256,1024]{2,1,0:T(8,128)(2,1)} %copy-done.7) | copy-start | bytes 3145732
  132.6 2.8 %copy-start.6 = (bf16[2,256,1024]{2,1,0:T(8,128)(2,1)S(1)}, bf16[2,256,1024]{2,1,0:T(8,128)(2,1)}, u32[]{:S(2)}) copy-start(bf16[2,256,1024]{2,1,0:T(8,128)(2,1)} %copy-done.5) | copy-start | bytes 3145732
  132.6 2.8 %copy-start.18 = (bf16[4,256,2048]{2,1,0:T(8,128)(2,1)S(1)}, bf16[4,256,2048]{2,1,0:T(8,128)(2,1)}, u32[]{:S(2)}) copy-start(bf16[4,256,2048]{2,1,0:T(8,128)(2,1)} %get-tuple-element.18) | copy-start | bytes 12582916
  134.9 6.6 %collective-permute-start.4 = (bf16[512,512]{1,0:T(8,128)(2,1)S(1)}, bf16[512,512]{1,0:T(8,128)(2,1)S(1)}, u32[]{:S(2)}, u32[]{:S(2)}) collective-permute-start(bf16[512,512]{1,0:T(8,128)(2,1)S(1)} %bitcast.38), channel_id=1, source_target_pairs={{0,16},{16,0},{1,17},{17,1},{2,18},{18,2},{3,19},{19,3},{4,20},{20... | collective-permute-start | bytes 1572872 | tf_op jit(solution)/shard_map/ppermute | solution.py:243
  210.7 34.8 %copy-start.11 = (bf16[64,1024]{1,0:T(8,128)(2,1)S(1)}, bf16[64,1024]{1,0:T(8,128)(2,1)}, u32[]{:S(2)}) copy-start(bf16[64,1024]{1,0:T(8,128)(2,1)} %param.15) | copy-start | bytes 393220
  240.8 5.9 %collective-permute-start.5 = (bf16[64,2560]{1,0:T(8,128)(2,1)S(1)}, bf16[64,2560]{1,0:T(8,128)(2,1)S(1)}, u32[]{:S(2)}, u32[]{:S(2)}) collective-permute-start(bf16[64,2560]{1,0:T(8,128)(2,1)S(1)} %bitcast.33), channel_id=1, source_target_pairs={{0,16},{16,0},{1,17},{17,1},{2,18},{18,2},{3,19},{19,3},{4,20},{20... | collective-permute-start | bytes 983048 | tf_op jit(solution)/shard_map/ppermute | solution.py:243
  249.7 11.4 %all-to-all-start.4 = ((f32[16,8,128]{2,1,0:T(8,128)}), f32[16,8,128]{2,1,0:T(8,128)S(1)}, u32[]{:S(2)}, u32[]{:S(2)}) async-start(f32[16,8,128]{2,1,0:T(8,128)} %reshape.161), calls=%async_computation.4 | async-start | bytes 131072 | tf_op jit(solution)/shard_map/all_to_all | solution.py:253
  262.9 1.8 copy-start.15
  265.0 2.7 copy-start.12
  265.0 2.7 copy-start.13
  267.7 2.6 copy-start.9
  267.7 2.6 copy-start.10
  (5 other events, 7.3 us)
Sparse Core Ops, SparseCore 0:
  23.8 84.2 all-gather.1
